TPU v7x, 128 devices: a whole 4x4x4 slice. The times are simulated.
128 devices in a mesh: dp: 4 (over y), mp: 32 (over x, z, core).
Axes of the slice: x: 4, y: 4, z: 4, core: 2. Of those that a mesh axis runs over, the one named last changes fastest.
Arguments:
- residual_in: bfloat16 [512, 3584], P('dp', 'mp'), may hold values from -6 to 6
- pre_gain: float32 [3584], replicated, may hold values from 0.5 to 1.5
- post_gain: float32 [3584], replicated, may hold values from 0.5 to 1.5
- w_gate: bfloat16 [3584, 14336], P(None, 'mp'), may hold values from -0.09375 to 0.09375
- w_up: bfloat16 [3584, 14336], P(None, 'mp'), may hold values from -0.09375 to 0.09375
- w_down: bfloat16 [14336, 3584], P('mp'), may hold values from -0.046875 to 0.046875
- w_enc: bfloat16 [3584, 65536], P(None, ('dp', 'mp')), may hold values from -0.09375 to 0.09375
- b_enc: float32 [65536], P(('dp', 'mp')), may hold values from -2.5 to 2.5
- threshold: float32 [65536], P(('dp', 'mp')), may hold values from 0.1 to 1
- w_dec: bfloat16 [65536, 3584], P(('dp', 'mp')), may hold values from -0.0234375 to 0.0234375
- b_dec: float32 [3584], replicated, may hold values from -1.5 to 1.5
Outputs:
- loss_value: float32 [], replicated
- d_w_enc: bfloat16 [3584, 65536], P(None, ('dp', 'mp'))
- d_w_dec: bfloat16 [65536, 3584], P(('dp', 'mp'))
- d_b_enc: float32 [65536], P(('dp', 'mp'))
- d_threshold: float32 [65536], P(('dp', 'mp'))
- d_b_dec: float32 [3584], replicated
All inputs are finite; a program needn't handle non-finite values.
Results may differ from a plain program's by a relative error of at most 0.014.
The roundings to bfloat16 on the way count: a program that leaves them out, or rounds other values in their place, can miss the bound.
Values may be sent and summed in bfloat16 or wider, within the bound.
A program may use at most 128 MiB of HBM per device.

v0:
```python
import jax
import jax.numpy as jnp
from jax import lax
from jax.sharding import PartitionSpec as P

norm_eps = 1e-06
gate_band = 0.1
sparsity_coef = 0.05


def contract_first(left, right):
    return lax.dot_general(
        left, right, (((0,), (0,)), ((), ())), preferred_element_type=jnp.float32
    )


def local(
    residual_in, pre_gain, post_gain, w_gate, w_up, w_down, w_enc, b_enc, threshold, w_dec, b_dec
):
    full_rows = lax.all_gather(residual_in, "mp", axis=1, tiled=True)
    resid_wide = full_rows.astype(jnp.float32)
    normed = (
        resid_wide
        * lax.rsqrt(jnp.mean(resid_wide * resid_wide, axis=1, keepdims=True) + norm_eps)
        * pre_gain[None, :]
    ).astype(jnp.bfloat16)
    gate_out = jnp.dot(normed, w_gate, preferred_element_type=jnp.float32)
    up_out = jnp.dot(normed, w_up, preferred_element_type=jnp.float32)
    hidden = (jax.nn.gelu(gate_out, approximate=True) * up_out).astype(jnp.bfloat16)
    col_width = residual_in.shape[1]
    model_width = full_rows.shape[1]
    out_share = lax.psum_scatter(
        lax.dot_general(
            w_down, hidden, (((0,), (1,)), ((), ())), preferred_element_type=jnp.float32
        ),
        "mp",
        scatter_dimension=0,
        tiled=True,
    )
    total_sq = lax.psum(jnp.sum(out_share * out_share, axis=0), "mp")
    row_scale = lax.rsqrt(total_sq / model_width + norm_eps)
    my_cols = lax.axis_index("mp") * col_width
    gain_share = lax.dynamic_slice_in_dim(post_gain, my_cols, col_width, 0)
    mixed = residual_in.T.astype(jnp.float32) + out_share * row_scale[None, :] * gain_share[:, None]
    column_rows = lax.all_gather(mixed.astype(jnp.bfloat16), "mp", axis=0, tiled=True)
    h_cols = lax.all_gather(column_rows, "dp", axis=1, tiled=True)
    pre_act = contract_first(h_cols, w_enc) + b_enc[None, :]
    soft = jax.nn.sigmoid((pre_act - threshold[None, :]) / gate_band)
    feat_bf = (pre_act * soft).astype(jnp.bfloat16)
    gate_part = jnp.sum(soft)
    recon_part = lax.dot_general(
        w_dec, feat_bf, (((0,), (1,)), ((), ())), preferred_element_type=jnp.float32
    )
    recon_all, gate_total = lax.psum((recon_part, gate_part), ("dp", "mp"))
    error_t = recon_all + b_dec[:, None] - h_cols.astype(jnp.float32)
    grad_bdec = jnp.sum(error_t, axis=1)
    square_total = jnp.sum(error_t * error_t)
    err_bf = error_t.astype(jnp.bfloat16)
    loss_value = (0.5 * square_total + sparsity_coef * gate_total) / (
        h_cols.shape[0] * h_cols.shape[1]
    )
    grad_wdec = lax.dot_general(
        feat_bf, err_bf, (((0,), (1,)), ((), ())), preferred_element_type=jnp.float32
    ).astype(jnp.bfloat16)
    grad_feat = lax.dot_general(
        err_bf, w_dec, (((0,), (1,)), ((), ())), preferred_element_type=jnp.float32
    )
    slope = soft * (1.0 - soft) / gate_band
    side_term = (grad_feat * pre_act + sparsity_coef) * slope
    grad_pre = grad_feat * soft + side_term
    grad_thresh = -jnp.sum(side_term, axis=0)
    grad_benc = jnp.sum(grad_pre, axis=0)
    grad_wenc = jnp.dot(
        h_cols, grad_pre.astype(jnp.bfloat16), preferred_element_type=jnp.float32
    ).astype(jnp.bfloat16)
    return (loss_value, grad_wenc, grad_wdec, grad_benc, grad_thresh, grad_bdec)


def solution(mesh):
    placed = (
        P("dp", "mp"),
        P(),
        P(),
        P(None, "mp"),
        P(None, "mp"),
        P("mp", None),
        P(None, ("dp", "mp")),
        P(("dp", "mp")),
        P(("dp", "mp")),
        P(("dp", "mp"), None),
        P(),
    )
    return jax.shard_map(
        local,
        mesh=mesh,
        in_specs=placed,
        out_specs=(
            P(),
            P(None, ("dp", "mp")),
            P(("dp", "mp"), None),
            P(("dp", "mp")),
            P(("dp", "mp")),
            P(),
        ),
        check_vma=False,
    )
```

profile of v0, /device:TPU:1, one launch (start us, length us, event | category | flops | bytes accessed | tf_op | source)
XLA Modules:
  0.0 526.1 jit_solution(124205612583446622)
XLA Ops:
  7.2 0.0 copy-start
  7.2 0.0 reduce-scatter.4.cloned.1.call-start
  7.2 27.9 %all_gather.9 = bf16[128,3584]{0,1:T(8,128)(2,1)S(1)} all-gather(bf16[128,112]{0,1:T(8,128)(2,1)} %param.11), channel_id=1, replica_groups=mesh['dp'=4,'mp'=32] {'mp'}, dimensions={1}, use_global_device_ids=true | all-gather | bytes 946176 | tf_op jit(solution)/shard_map/all_gather | solution.py:20
  35.1 0.0 copy-start.1
  35.1 0.0 copy-start.3
  35.1 0.5 fusion.2
  35.6 0.4 copy-done.1
  36.0 3.1 fusion.20
  39.1 0.0 copy-done
  39.1 0.0 copy-done.3
  39.1 6.0 %convolution_bitcast_fusion.1 = f32[3584,128]{0,1:T(8,128)} fusion(bf16[448,3584]{1,0:T(8,128)(2,1)S(1)} %copy-done, f32[128,448]{0,1:T(8,128)S(1)} %fusion.20, bf16[3584,448]{0,1:T(8,128)(2,1)} %param.15, bf16[128,3584]{0,1:T(8,128)(2,1)} %copy-done.1, f32[3584]{0:T(1024)S(1)} %copy-done.3, f32[128]{0:T(128)S(1)} %add_rsqrt_fusion.1), kind=kOutput, calls=%fused_computation.5 | convolution fusion | flops 824033280 | bytes 9419264 | tf_op jit(solution)/shard_map/dot_general | solution.py:33
  45.1 0.0 copy-start.2
  45.1 2.7 copy.23
  47.8 0.0 copy-start.7
  47.8 0.0 reduce-scatter.4.cloned.1.call-update
  47.8 0.0 all-gather.2.cloned.1.call-start
  47.9 0.8 dynamic_slice.3
  48.6 75.3 %reduce-scatter.4.cloned.1.call-done = f32[112,128]{1,0:T(8,128)} async-done(((f32[3584,128]{1,0:T(8,128)}), f32[112,128]{1,0:T(8,128)}) %reduce-scatter.4.cloned.1.call-update) | async-done | bytes 57360 | tf_op jit(solution)/shard_map/reduce_scatter | solution.py:32
  123.9 0.9 copy.24
  124.8 0.1 multiply_reduce_fusion.1
  124.9 64.3 %psum.21 = f32[128]{0:T(128)S(1)} all-reduce(f32[128]{0:T(128)S(1)} %multiply_reduce_fusion.1), channel_id=1, replica_groups=mesh['dp'=4,'mp'=32] {'mp'}, use_global_device_ids=true, to_apply=%region_3.0 | all-reduce | flops 128 | bytes 1024 | tf_op jit(solution)/shard_map/psum | solution.py:40
  189.3 0.0 copy-done.2
  189.3 0.9 fusion.23
  190.2 25.7 %all_gather.10 = bf16[3584,128]{1,0:T(8,128)(2,1)} all-gather(bf16[112,128]{1,0:T(8,128)(2,1)S(1)} %fusion.23), channel_id=1, replica_groups=mesh['dp'=4,'mp'=32] {'mp'}, dimensions={0}, use_global_device_ids=true | all-gather | bytes 946176 | tf_op jit(solution)/shard_map/all_gather | solution.py:45
  215.9 2.2 copy.22
  218.1 0.0 all-gather.2.cloned.1.call-update
  218.1 0.0 copy-start.8
  218.1 0.2 all-reduce.2.cloned.1.call-start
  218.3 42.6 %all-gather.2.cloned.1.call-done = bf16[3584,512]{0,1:T(8,128)(2,1)} async-done(((bf16[3584,128]{0,1:T(8,128)(2,1)}), bf16[3584,512]{0,1:T(8,128)(2,1)}) %all-gather.2.cloned.1.call-update) | async-done | bytes 3670032 | tf_op jit(solution)/shard_map/all_gather | solution.py:46
  260.9 0.0 copy-done.7
  260.9 5.3 %convolution_add_fusion = f32[512,512]{1,0:T(8,128)S(1)} fusion(bf16[3584,512]{0,1:T(8,128)(2,1)} %all-gather.2.cloned.1.call-done, bf16[3584,512]{1,0:T(8,128)(2,1)} %param.17, f32[512]{0:T(512)S(1)} %copy-done.7), kind=kOutput, calls=%fused_computation.14 | convolution fusion | flops 1879310336 | bytes 8390656 | tf_op jit(solution)/shard_map/dot_general | solution.py:12
  266.3 0.0 copy-start.9
  266.3 1.0 copy-done.9
  267.2 0.0 copy-done.8
  267.2 0.0 copy-done.5
  267.2 5.1 convolution_bitcast_fusion
  272.4 0.0 all-reduce.2.cloned.1.call-update
  272.4 160.2 %all-reduce.2.cloned.1.call-done = f32[3584,512]{0,1:T(8,128)} async-done(((f32[3584,512]{0,1:T(8,128)}), f32[3584,512]{0,1:T(8,128)}) %all-reduce.2.cloned.1.call-update) | async-done | bytes 7340048 | tf_op jit(solution)/shard_map/psum | solution.py:54
  432.6 0.0 copy-done.4
  432.6 0.0 copy-start.10
  432.6 5.9 %fusion = (f32[3584]{0:T(1024)}, f32[]{:T(128)}, bf16[3584,512]{0,1:T(8,128)(2,1)S(1)}) fusion(bf16[3584,512]{0,1:T(8,128)(2,1)} %all-gather.2.cloned.1.call-done, f32[3584,512]{0,1:T(8,128)} %all-reduce.2.cloned.1.call-done, f32[3584]{0:T(1024)S(1)} %copy-done.4), kind=kLoop, calls=%fused_computation.8 | loop fusion | flops 12841471 | bytes 14708740 | tf_op jit(solution)/shard_map/reduce_sum | solution.py:56
  438.6 0.0 copy-done.6
  438.6 0.0 copy-done.10
  438.6 3.9 fusion.25
  442.4 4.0 convolution_convert_fusion
  446.4 64.1 %psum.23 = f32[]{:T(128)} all-reduce(f32[]{:T(128)} %get-tuple-element.13), channel_id=1, replica_groups=mesh['dp'=4,'mp'=32] {'dp','mp'}, use_global_device_ids=true, to_apply=%region_7.0 | all-reduce | flops 1 | bytes 8 | tf_op jit(solution)/shard_map/psum | solution.py:54
  510.5 0.6 neg.7
  512.4 6.1 %convolution_convert_fusion.1 = bf16[3584,512]{1,0:T(8,128)(2,1)} fusion(bf16[3584,512]{0,1:T(8,128)(2,1)} %all-gather.2.cloned.1.call-done, bf16[512,512]{1,0:T(8,128)(2,1)} %get-tuple-element.11), kind=kOutput, calls=%fused_computation.4 | convolution fusion | flops 1880883200 | bytes 7864320 | tf_op jit(solution)/shard_map/dot_general | solution.py:73
  (5 shorter events, 0.0 us)
Async XLA Ops:
  7.2 31.9 %copy-start = (bf16[448,3584]{1,0:T(8,128)(2,1)S(1)}, bf16[448,3584]{1,0:T(8,128)(2,1)}, u32[]{:S(2)}) copy-start(bf16[448,3584]{1,0:T(8,128)(2,1)} %param.16) | copy-start | bytes 9633796
  7.2 116.7 %reduce-scatter.4.cloned.1.call-start = ((), (), s32[]{:S(2)}) async-start(), calls=%async_computation.3 | async-start | bytes 1892352 | tf_op jit(solution)/shard_map/reduce_scatter | solution.py:32
  35.1 0.9 copy-start.1
  35.1 4.0 copy-start.3
  45.1 144.2 %copy-start.2 = (bf16[128,112]{0,1:T(8,128)(2,1)S(1)}, bf16[128,112]{0,1:T(8,128)(2,1)}, u32[]{:S(2)}) copy-start(bf16[128,112]{0,1:T(8,128)(2,1)} %param.11) | copy-start | bytes 86020
  47.8 213.1 %copy-start.7 = (f32[512]{0:T(512)S(1)}, f32[512]{0:T(512)}, u32[]{:S(2)}) copy-start(f32[512]{0:T(512)} %param.18) | copy-start | bytes 6148
  47.8 213.1 %all-gather.2.cloned.1.call-start = ((), (), s32[]{:S(2)}) async-start(), calls=%async_computation.1 | async-start | bytes 4587520 | tf_op jit(solution)/shard_map/all_gather | solution.py:46
  218.1 49.1 %copy-start.8 = (f32[512]{0:T(512)S(1)}, f32[512]{0:T(512)}, u32[]{:S(2)}) copy-start(f32[512]{0:T(512)} %param.19) | copy-start | bytes 6148
  218.1 214.5 %all-reduce.2.cloned.1.call-start = ((), (), s32[]{:S(2)}) async-start(), calls=%async_computation.2 | async-start | bytes 14680064 | tf_op jit(solution)/shard_map/psum | solution.py:54
  260.9 6.3 %copy-start.5 = (bf16[512,3584]{1,0:T(8,128)(2,1)S(1)}, bf16[512,3584]{1,0:T(8,128)(2,1)}, u32[]{:S(2)}) copy-start(bf16[512,3584]{1,0:T(8,128)(2,1)} %param.20) | copy-start | bytes 11010052
  266.3 1.0 copy-start.9
  272.4 160.2 %copy-start.4 = (f32[3584]{0:T(1024)S(1)}, f32[3584]{0:T(1024)}, u32[]{:S(2)}) copy-start(f32[3584]{0:T(1024)} %param.21) | copy-start | bytes 43012
  432.6 6.0 %copy-start.6 = (bf16[512,3584]{1,0:T(8,128)(2,1)S(1)}, bf16[512,3584]{1,0:T(8,128)(2,1)}, u32[]{:S(2)}) copy-start(bf16[512,3584]{1,0:T(8,128)(2,1)} %param.20) | copy-start | bytes 11010052
  432.6 6.0 %copy-start.10 = (f32[512,512]{1,0:T(8,128)S(1)}, f32[512,512]{1,0:T(8,128)}, u32[]{:S(2)}) copy-start(f32[512,512]{1,0:T(8,128)} %copy-done.9) | copy-start | bytes 3145732
Sparse Core Ops, SparseCore 0:
  47.9 75.9 reduce-scatter.3
  218.2 42.6 all-gather.1
  272.5 160.0 all-reduce.1
where the time goes:
time: 527 us; the launch traced here: 526 us
  waiting for transfers between devices  278 us (53%)
  blocking collectives  182 us (35%)
  matrix products  33.4 us (6%)
  between operations  16.3 us (3%)
  local copies, waits for them, and re-layouts  8.05 us (2%)
  other arithmetic  8.04 us (2%)
    psum x1, waiting for transfers between devices, local(): recon_all, gate_total = lax.psum((recon_part, gate_part), ('dp', 'mp'))  160 us
    reduce_scatter x1, waiting for transfers between devices, local(): lax.psum_scatter(lax.dot_general(w_down, hidden, (((0,), (1,)), ((), ()))...  75.3 us
    psum x1, blocking collectives, local(): total_sq = lax.psum(jnp.sum(out_share * out_share, axis=0), 'mp')  64.3 us
    psum x1, blocking collectives, local(): recon_all, gate_total = lax.psum((recon_part, gate_part), ('dp', 'mp'))  64.1 us
    all_gather x1, waiting for transfers between devices, local(): h_cols = lax.all_gather(column_rows, 'dp', axis=1, tiled=True)  42.6 us
    all_gather x1, blocking collectives, local(): full_rows = lax.all_gather(residual_in, 'mp', axis=1, tiled=True)  27.9 us
    all_gather x1, blocking collectives, local(): lax.all_gather(mixed.astype(jnp.bfloat16), 'mp', axis=0, tiled=True)  25.7 us
  transfers between devices with their start and end apart: 3, of which 3 were waited for; matrix products, arithmetic and copies ran while one was open for 0% of the time, Pallas kernels for 0%

commit v1 on v0

v1 whole, which is shorter than its diff:
```python
import jax
import jax.numpy as jnp
from jax import lax
from jax.experimental import pallas as pl
from jax.experimental.pallas import tpu as pltpu
from jax.sharding import PartitionSpec as P

norm_eps = 1e-06
gate_band = 0.1
sparsity_coef = 0.05

MESH = pl.DeviceIdType.MESH
F32 = jnp.float32
BF16 = jnp.bfloat16

D = 3584
QUARTER = 896
WIDTHS = (256, 256, 384)
OFFSETS = (0, 256, 512)
ORDERS = ("xyz", "yzx", "zxy")
PIECES = (0, 1, 2)


def coordinates():
    y = lax.axis_index("dp")
    m = lax.axis_index("mp")
    return {"x": m // 8, "y": y, "z": (m // 2) % 4, "c": m % 2}


def device(at):
    return (at["y"], (at["x"] * 4 + at["z"]) * 2 + at["c"])


def moved(at, axis, steps):
    there = dict(at)
    there[axis] = (at[axis] + steps) % (2 if axis == "c" else 4)
    return there


def grid_index(at, gathered):
    return tuple(slice(None) if a in gathered else at[a] for a in "yxz")


def mlp_and_sae(
    resid, pre_gain, post_gain, b_dec, b_enc, threshold,
    wg_hbm, wu_hbm, wd_hbm, we_hbm, wdec_hbm,
    err_out0, err_out1, err_out2, l_out0, l_out1, l_out2, feat_out, pre_out, gate_out,
    wg, wu, wd, we, wdec, gath, norm_t, hidden, bp, bp_in, bs, b_in, sq, sq_in,
    l0, l1, l2, feat, pre, p0, p1, p2, pin0, pin1, pin2, s0, s1, s2,
    ra0, ra1, ra2, sa0, sa1, sa2, rb0, rb1, rb2, sb0, sb1, sb2, rc0, rc1, rc2,
    e0, e1, e2, gsum, gin,
    wsem, asend, arecv, bcsend, bcrecv, bsend, brecv, sqsend, sqrecv,
    dsend, drecv, dcsend, dcrecv, pcsend, pcrecv, rsend, rrecv,
    esend, erecv, ecsend, ecrecv, gsend, grecv, osem,
):
    at = coordinates()
    x, y, z, c = at["x"], at["y"], at["z"], at["c"]
    sibling = device(moved(at, "c", 1))
    layer = (l0, l1, l2)
    part = (p0, p1, p2)
    part_in = (pin0, pin1, pin2)
    total = (s0, s1, s2)
    in_a, sum_a = (ra0, ra1, ra2), (sa0, sa1, sa2)
    in_b, sum_b = (rb0, rb1, rb2), (sb0, sb1, sb2)
    in_c = (rc0, rc1, rc2)
    err = (e0, e1, e2)

    loads = [
        pltpu.make_async_copy(src, dst, wsem.at[i])
        for i, (src, dst) in enumerate(
            ((wg_hbm, wg), (wu_hbm, wu), (wd_hbm, wd), (we_hbm, we), (wdec_hbm, wdec))
        )
    ]
    for load in loads:
        load.start()

    plane = [(i, j) for i in range(4) for j in range(4) if i or j]
    barrier = pltpu.get_barrier_semaphore()
    greeted = [moved(moved(at, "x", i), "z", j) for i, j in plane]
    greeted += [moved(at, "y", k) for k in (1, 2, 3)] + [moved(at, "c", 1)]
    for there in greeted:
        pl.semaphore_signal(barrier, inc=1, device_id=device(there), device_id_type=MESH)
    pl.semaphore_wait(barrier, len(greeted))

    def remote(src, dst, send, recv, there):
        copy = pltpu.make_async_remote_copy(
            src_ref=src, dst_ref=dst, send_sem=send, recv_sem=recv,
            device_id=there, device_id_type=MESH,
        )
        copy.start()
        return copy

    unsent = []

    copies = []
    for n, (i, j) in enumerate(plane):
        there = moved(moved(at, "x", i), "z", j)
        copies.append(remote(resid, gath.at[x, z, c], asend.at[n], arecv.at[n], device(there)))
    gath[x, z, c] = resid[...]
    for copy in copies:
        copy.wait_recv()
    unsent += copies
    copy = remote(gath.at[:, :, c], gath.at[:, :, c], asend.at[15], arecv.at[15], sibling)
    copy.wait_recv()
    unsent.append(copy)

    squares = jnp.zeros((1, 128), F32)
    for i in range(4):
        for j in range(4):
            rows = gath[i, j].astype(F32).reshape(224, 128)
            squares = squares + jnp.sum(rows * rows, axis=0, keepdims=True)
    scale = lax.rsqrt(squares / D + norm_eps)
    gains = jnp.concatenate([pre_gain[...], jnp.zeros((100, 128), F32)], axis=0).T
    everything = gath[...].reshape(D, 128)
    for k in range(28):
        rows = everything[k * 128:(k + 1) * 128].astype(F32)
        norm_t[k * 128:(k + 1) * 128, :] = (rows * scale * gains[:, k:k + 1]).astype(BF16)

    loads[0].wait()
    loads[1].wait()
    gate = jnp.dot(wg[...], norm_t[...], preferred_element_type=F32)
    up = jnp.dot(wu[...], norm_t[...], preferred_element_type=F32)
    hidden[...] = (jax.nn.gelu(gate, approximate=True) * up).T.astype(BF16)

    loads[2].wait()
    copies = []
    for q in range(4):
        own = jnp.dot(hidden[...], wd[:, q * QUARTER:(q + 1) * QUARTER], preferred_element_type=F32)
        bp[:, :, q] = own.astype(BF16).reshape(2, 4, 16, QUARTER)
        copies.append(remote(bp.at[1 - c, :, q], bp_in.at[:, q], bcsend.at[q], bcrecv.at[q], sibling))
    for q, copy in enumerate(copies):
        copy.wait_recv()
        bs[:, q] = (bp[c, :, q].astype(F32) + bp_in[:, q].astype(F32)).astype(BF16)
    unsent += copies
    copies = []
    for n, (i, j) in enumerate(plane):
        there = moved(moved(at, "x", i), "z", j)
        copies.append(
            remote(bs.at[there["x"], there["z"]], b_in.at[n], bsend.at[n], brecv.at[n], device(there))
        )
    pick = lax.broadcasted_iota(jnp.int32, (16, 128), 0) + (c * 64 + x * 16)
    pick = (lax.broadcasted_iota(jnp.int32, (16, 128), 1) == pick).astype(BF16)
    mine = lax.dot_general(
        pick, own_rows(gath, z), (((1,), (1,)), ((), ())), preferred_element_type=F32
    )
    block = bs[x, z].astype(F32)
    for n, copy in enumerate(copies):
        copy.wait_recv()
        block = block + b_in[n].astype(F32)
    unsent += copies
    sums = jnp.broadcast_to(jnp.sum(block * block, axis=1, keepdims=True), (16, 128))
    sq[...] = sums
    copies = [
        remote(sq, sq_in.at[k - 1], sqsend.at[k - 1], sqrecv.at[k - 1], device(moved(at, "z", k)))
        for k in (1, 2, 3)
    ]
    for k, copy in enumerate(copies):
        copy.wait_recv()
        sums = sums + sq_in[k]
    unsent += copies
    row_scale = lax.rsqrt(sums[:, :1] / D + norm_eps)
    gain = lane_row(post_gain, z)
    block = mine + block * row_scale * gain
    for p in PIECES:
        layer[p][c, y, x, z] = block[:, OFFSETS[p]:OFFSETS[p] + WIDTHS[p]].astype(BF16)

    def gather(arrays, send, recv, csend, crecv):
        held = []
        stage = {}
        for step in range(3):
            for p in PIECES:
                order = ORDERS[p]
                if step:
                    for copy in stage[p]:
                        copy.wait_recv()
                here = arrays[p].at[(c,) + grid_index(at, order[:step])]
                stage[p] = [
                    remote(here, here, send.at[step, p, k - 1], recv.at[step, p, k - 1],
                           device(moved(at, order[step], k)))
                    for k in (1, 2, 3)
                ]
                held.extend(stage[p])
                if step == 2:
                    held.append(remote(here, here, csend.at[p, 0], crecv.at[p, 0], sibling))
        across = [copy for copy in held[-12:][3::4]]
        for k in (1, 2, 3):
            for p in PIECES:
                order = ORDERS[p]
                stage[p][k - 1].wait_recv()
                source = moved(at, order[2], -k)
                there = arrays[p].at[(c,) + grid_index(source, order[:2])]
                copy = remote(there, there, csend.at[p, k], crecv.at[p, k], sibling)
                held.append(copy)
                across.append(copy)
        for copy in across:
            copy.wait_recv()
        return held

    unsent += gather(layer, dsend, drecv, dcsend, dcrecv)
    outs = [
        pltpu.make_async_copy(layer[p], (l_out0, l_out1, l_out2)[p], osem.at[p]) for p in PIECES
    ]
    for out in outs:
        out.start()

    loads[3].wait()
    pre[...] = jnp.broadcast_to(b_enc[...], (512, 512))
    for q in range(4):
        for p in PIECES:
            low = q * QUARTER + OFFSETS[p]
            rows = layer[p][:, :, :, q].reshape(512, WIDTHS[p])
            pre[...] += jnp.dot(rows, we[low:low + WIDTHS[p], :], preferred_element_type=F32)
    pre_act = pre[...]
    soft = jax.nn.sigmoid((pre_act - threshold[...]) / gate_band)
    feat[...] = (pre_act * soft).astype(BF16)
    gate_sum = jnp.broadcast_to(jnp.sum(soft).reshape(1, 1), (8, 128))
    outs.append(pltpu.make_async_copy(feat, feat_out, osem.at[3]))
    outs.append(pltpu.make_async_copy(pre, pre_out, osem.at[4]))
    outs[3].start()
    outs[4].start()

    loads[4].wait()

    def partial(half):
        rows = feat[pl.ds(pl.multiple_of(half * 256, 256), 256), :]
        for q in range(4):
            for p in PIECES:
                low = q * QUARTER + OFFSETS[p]
                value = jnp.dot(rows, wdec[:, low:low + WIDTHS[p]], preferred_element_type=F32)
                part[p][half, :, :, q] = value.astype(BF16).reshape(4, 4, 16, WIDTHS[p])

    partial(1 - c)
    copies = [
        remote(part[p].at[1 - c], part_in[p], pcsend.at[p], pcrecv.at[p], sibling) for p in PIECES
    ]
    unsent += copies
    gsum[0] = gate_sum
    gate_copies = [remote(gsum.at[0], gin.at[9], gsend.at[9], grecv.at[9], sibling)]
    partial(c)
    stage = {}
    for p in PIECES:
        copies[p].wait_recv()
        for i in range(4):
            total[p][i] = (part[p][c, i].astype(F32) + part_in[p][i].astype(F32)).astype(BF16)
        axis = ORDERS[p][2]
        stage[p] = []
        for k in (1, 2, 3):
            there = moved(at, axis, k)
            src = total[p].at[grid_index(there, [a for a in "xyz" if a != axis])]
            stage[p].append(
                remote(src, in_a[p].at[k - 1], rsend.at[0, p, k - 1], rrecv.at[0, p, k - 1], device(there))
            )
        unsent += stage[p]
    gate_copies[0].wait_recv()
    gate_sum = gate_sum + gin[9]
    unsent += gate_copies

    def gate_step(s, axis, value):
        gsum[1 + s] = value
        made = [
            remote(gsum.at[1 + s], gin.at[3 * s + k - 1], gsend.at[3 * s + k - 1],
                   grecv.at[3 * s + k - 1], device(moved(at, axis, k)))
            for k in (1, 2, 3)
        ]
        return made

    def gate_finish(s, made, value):
        for k, copy in enumerate(made):
            copy.wait_recv()
            value = value + gin[3 * s + k]
        return value

    gate_copies = gate_step(0, "x", gate_sum)
    unsent += gate_copies
    for p in PIECES:
        last, second = ORDERS[p][2], ORDERS[p][1]
        for copy in stage[p]:
            copy.wait_recv()
        value = total[p][grid_index(at, [a for a in "xyz" if a != last])].astype(F32)
        for k in range(3):
            value = value + in_a[p][k].astype(F32)
        sum_a[p][...] = value.astype(BF16)
        stage[p] = []
        left = [a for a in "yxz" if a != last]
        for k in (1, 2, 3):
            there = moved(at, second, k)
            src = sum_a[p].at[tuple(there[a] if a == second else slice(None) for a in left)]
            stage[p].append(
                remote(src, in_b[p].at[k - 1], rsend.at[1, p, k - 1], rrecv.at[1, p, k - 1], device(there))
            )
        unsent += stage[p]
    gate_sum = gate_finish(0, gate_copies, gate_sum)
    gate_copies = gate_step(1, "y", gate_sum)
    unsent += gate_copies
    for p in PIECES:
        last, second, first = ORDERS[p][2], ORDERS[p][1], ORDERS[p][0]
        for copy in stage[p]:
            copy.wait_recv()
        left = [a for a in "yxz" if a != last]
        value = sum_a[p][tuple(at[a] if a == second else slice(None) for a in left)].astype(F32)
        for k in range(3):
            value = value + in_b[p][k].astype(F32)
        sum_b[p][...] = value.astype(BF16)
        stage[p] = []
        for k in (1, 2, 3):
            there = moved(at, first, k)
            stage[p].append(
                remote(sum_b[p].at[there[first]], in_c[p].at[k - 1], rsend.at[2, p, k - 1],
                       rrecv.at[2, p, k - 1], device(there))
            )
        unsent += stage[p]
    gate_sum = gate_finish(1, gate_copies, gate_sum)
    gate_copies = gate_step(2, "z", gate_sum)
    unsent += gate_copies
    bias = lane_row(b_dec, z)
    for p in PIECES:
        for copy in stage[p]:
            copy.wait_recv()
        value = sum_b[p][at[ORDERS[p][0]]].astype(F32)
        for k in range(3):
            value = value + in_c[p][k].astype(F32)
        value = value + bias[:, OFFSETS[p]:OFFSETS[p] + WIDTHS[p]]
        value = value - layer[p][c, y, x, z].astype(F32)
        err[p][c, y, x, z] = value.astype(BF16)

    unsent += gather(err, esend, erecv, ecsend, ecrecv)
    gate_sum = gate_finish(2, gate_copies, gate_sum)
    gate_out[...] = gate_sum
    for p in PIECES:
        out = pltpu.make_async_copy(err[p], (err_out0, err_out1, err_out2)[p], osem.at[5 + p])
        out.start()
        outs.append(out)
    for copy in unsent:
        copy.wait_send()
    for out in outs:
        out.wait()


def own_rows(gath, z):
    return gath[pl.ds(z, 1)].reshape(QUARTER, 128)


def lane_row(ref, z):
    rows = [ref[pl.ds(z * 7 + i, 1), :] for i in range(7)]
    return jnp.concatenate(rows, axis=1)


def gradients(
    threshold, gate_in,
    e0_hbm, e1_hbm, e2_hbm, l0_hbm, l1_hbm, l2_hbm, feat_hbm, pre_hbm, wdec_hbm,
    wenc_grad, wdec_grad, benc_grad, thresh_grad, bdec_grad, loss,
    e0, e1, e2, l0, l1, l2, feat, feat_t, pre, wdec, gfeat, gpre, odec, oenc,
    isem, dsem, esem,
):
    err = (e0, e1, e2)
    layer = (l0, l1, l2)
    pairs = (
        (feat_hbm, feat), (e0_hbm, e0), (e1_hbm, e1), (e2_hbm, e2), (wdec_hbm, wdec),
        (pre_hbm, pre), (l0_hbm, l0), (l1_hbm, l1), (l2_hbm, l2),
    )
    loads = [pltpu.make_async_copy(src, dst, isem.at[i]) for i, (src, dst) in enumerate(pairs)]
    for load in loads:
        load.start()
    loads[0].wait()
    feat_t[...] = feat[...].T
    loads[4].wait()
    square = jnp.zeros((1, 1), F32)
    stores = []
    for p in PIECES:
        loads[1 + p].wait()
        width = WIDTHS[p]
        for q in range(4):
            low = q * QUARTER + OFFSETS[p]
            rows = err[p][:, :, :, q].reshape(512, width)
            odec[:, low:low + width] = jnp.dot(
                feat_t[...], rows, preferred_element_type=F32
            ).astype(BF16)
            store = pltpu.make_async_copy(
                odec.at[:, pl.ds(low, width)], wdec_grad.at[:, pl.ds(low, width)], dsem.at[p * 4 + q]
            )
            store.start()
            stores.append(store)
            more = lax.dot_general(
                rows, wdec[:, low:low + width], (((1,), (1,)), ((), ())), preferred_element_type=F32
            )
            if p == 0 and q == 0:
                gfeat[...] = more
            else:
                gfeat[...] += more
            wide = rows.astype(F32)
            bdec_grad[:, low:low + width] = jnp.sum(wide, axis=0, keepdims=True)
            square = square + jnp.sum(jnp.sum(wide * wide, axis=0, keepdims=True), axis=1, keepdims=True)
    loss[...] = (0.5 * square + sparsity_coef * gate_in[0:1, 0:1]) / (512 * D)
    loads[5].wait()
    pre_act = pre[...]
    soft = jax.nn.sigmoid((pre_act - threshold[...]) / gate_band)
    slope = soft * (1.0 - soft) / gate_band
    grad_feat = gfeat[...]
    side = (grad_feat * pre_act + sparsity_coef) * slope
    grad_pre = grad_feat * soft + side
    thresh_grad[...] = -jnp.sum(side, axis=0, keepdims=True)
    benc_grad[...] = jnp.sum(grad_pre, axis=0, keepdims=True)
    gpre[...] = grad_pre.astype(BF16)
    for p in PIECES:
        loads[6 + p].wait()
        width = WIDTHS[p]
        for q in range(4):
            low = q * QUARTER + OFFSETS[p]
            rows = layer[p][:, :, :, q].reshape(512, width)
            oenc[low:low + width, :] = lax.dot_general(
                rows, gpre[...], (((0,), (0,)), ((), ())), preferred_element_type=F32
            ).astype(BF16)
            store = pltpu.make_async_copy(
                oenc.at[pl.ds(low, width), :], wenc_grad.at[pl.ds(low, width), :], esem.at[p * 4 + q]
            )
            store.start()
            stores.append(store)
    for store in stores:
        store.wait()


def blocks(dtype=BF16, lead=(2, 4, 4, 4)):
    return [pltpu.VMEM(lead + (16, w), dtype) for w in WIDTHS]


def local(
    residual_in, pre_gain, post_gain, w_gate, w_up, w_down, w_enc, b_enc, threshold, w_dec, b_dec
):
    vmem = pl.BlockSpec(memory_space=pltpu.VMEM)
    hbm = pl.BlockSpec(memory_space=pl.ANY)
    dma = pltpu.SemaphoreType.DMA
    shape = jax.ShapeDtypeStruct
    full = [shape((2, 4, 4, 4, 16, w), BF16) for w in WIDTHS]
    b_enc = b_enc.reshape(1, 512)
    threshold = threshold.reshape(1, 512)
    made = pl.pallas_call(
        mlp_and_sae,
        out_shape=full + full + [
            shape((512, 512), BF16), shape((512, 512), F32), shape((8, 128), F32),
        ],
        in_specs=[vmem] * 6 + [hbm] * 5,
        out_specs=[hbm] * 8 + [vmem],
        scratch_shapes=[
            pltpu.VMEM((448, D), BF16), pltpu.VMEM((448, D), BF16), pltpu.VMEM((448, D), BF16),
            pltpu.VMEM((D, 512), BF16), pltpu.VMEM((512, D), BF16),
            pltpu.VMEM((4, 4, 2, 112, 128), BF16), pltpu.VMEM((D, 128), BF16),
            pltpu.VMEM((128, 448), BF16),
            pltpu.VMEM((2, 4, 4, 16, QUARTER), BF16), pltpu.VMEM((4, 4, 16, QUARTER), BF16),
            pltpu.VMEM((4, 4, 16, QUARTER), BF16), pltpu.VMEM((15, 16, QUARTER), BF16),
            pltpu.VMEM((16, 128), F32), pltpu.VMEM((3, 16, 128), F32),
            *blocks(), pltpu.VMEM((512, 512), BF16), pltpu.VMEM((512, 512), F32),
            *blocks(), *blocks(lead=(4, 4, 4)), *blocks(lead=(4, 4, 4)),
            *blocks(lead=(3, 4, 4)), *blocks(lead=(4, 4)),
            *blocks(lead=(3, 4)), *blocks(lead=(4,)), *blocks(lead=(3,)),
            *blocks(), pltpu.VMEM((4, 8, 128), F32), pltpu.VMEM((10, 8, 128), F32),
            dma((5,)), dma((16,)), dma((16,)), dma((4,)), dma((4,)), dma((15,)), dma((15,)),
            dma((3,)), dma((3,)), dma((3, 3, 3)), dma((3, 3, 3)), dma((3, 4)), dma((3, 4)),
            dma((3,)), dma((3,)), dma((3, 3, 3)), dma((3, 3, 3)),
            dma((3, 3, 3)), dma((3, 3, 3)), dma((3, 4)), dma((3, 4)), dma((10,)), dma((10,)),
            dma((8,)),
        ],
        compiler_params=pltpu.CompilerParams(
            collective_id=0, has_side_effects=True, vmem_limit_bytes=56 * 1024 * 1024
        ),
        name="forward",
    )(
        residual_in.T, pre_gain.reshape(28, 128), post_gain.reshape(28, 128), b_dec.reshape(28, 128),
        b_enc, threshold, w_gate.T, w_up.T, w_down, w_enc, w_dec,
    )
    gate_total = made[8]
    grads = pl.pallas_call(
        gradients,
        out_shape=[
            shape((D, 512), BF16), shape((512, D), BF16), shape((1, 512), F32),
            shape((1, 512), F32), shape((1, D), F32), shape((1, 1), F32),
        ],
        in_specs=[vmem, vmem] + [hbm] * 9,
        out_specs=[hbm, hbm] + [vmem] * 4,
        scratch_shapes=[
            *blocks(), *blocks(), pltpu.VMEM((512, 512), BF16), pltpu.VMEM((512, 512), BF16),
            pltpu.VMEM((512, 512), F32), pltpu.VMEM((512, D), BF16), pltpu.VMEM((512, 512), F32),
            pltpu.VMEM((512, 512), BF16), pltpu.VMEM((512, D), BF16), pltpu.VMEM((D, 512), BF16),
            dma((9,)), dma((12,)), dma((12,)),
        ],
        compiler_params=pltpu.CompilerParams(vmem_limit_bytes=56 * 1024 * 1024),
        name="gradients",
    )(threshold, gate_total, *made[:8], w_dec)
    return (
        grads[5].reshape(()), grads[0], grads[1], grads[2].reshape(512), grads[3].reshape(512),
        grads[4].reshape(D),
    )


def solution(mesh):
    placed = (
        P("dp", "mp"),
        P(),
        P(),
        P(None, "mp"),
        P(None, "mp"),
        P("mp", None),
        P(None, ("dp", "mp")),
        P(("dp", "mp")),
        P(("dp", "mp")),
        P(("dp", "mp"), None),
        P(),
    )
    return jax.shard_map(
        local,
        mesh=mesh,
        in_specs=placed,
        out_specs=(
            P(),
            P(None, ("dp", "mp")),
            P(("dp", "mp"), None),
            P(("dp", "mp")),
            P(("dp", "mp")),
            P(),
        ),
        check_vma=False,
    )
```

time: 527 us -> 122 us (0.23)
  waiting for transfers between devices: 278 us -> 0 us
  blocking collectives: 182 us -> 0 us
  Pallas kernels: 0 us -> 119 us
  matrix products: 33.4 us -> 0 us
  between operations: 16.3 us -> 0.65 us
  local copies, waits for them, and re-layouts: 8.05 us -> 0 us
  other arithmetic: 8.04 us -> 1.36 us
    psum x1 -> x0, waiting for transfers between devices: 160 us -> none  [local(): recon_all, gate_total = lax.psum((recon_part, gate_part), ('dp', 'mp'))]
    psum x2 -> x0, blocking collectives: 128 us -> none  [the longest x1 64.3 us: local(): total_sq = lax.psum(jnp.sum(out_share * out_share, axis=0), 'mp')]
    pallas_call x0 -> x2, Pallas kernels: none -> 119 us  [the longest x1 105 us: local(): pl.pallas_call(mlp_and_sae, out_shape=full + full + [shape((512, 512), BF...]
    reduce_scatter x1 -> x0, waiting for transfers between devices: 75.3 us -> none  [local(): lax.psum_scatter(lax.dot_general(w_down, hidden, (((0,), (1,)), ((), ()))...]
    all_gather x2 -> x0, blocking collectives: 53.6 us -> none  [the longest x1 27.9 us: local(): full_rows = lax.all_gather(residual_in, 'mp', axis=1, tiled=True)]
    all_gather x1 -> x0, waiting for transfers between devices: 42.6 us -> none  [local(): h_cols = lax.all_gather(column_rows, 'dp', axis=1, tiled=True)]
    dot_general x7 -> x0, matrix products: 33.4 us -> none  [the longest x1 6.08 us: local(): jnp.dot(h_cols, grad_pre.astype(jnp.bfloat16), preferred_element_type=jnp...]
    reduce_sum x3 -> x0, other arithmetic: 6.54 us -> none  [the longest x1 5.95 us: local(): grad_bdec = jnp.sum(error_t, axis=1)]
  transfers between devices with their start and end apart: 3 -> 0, of which waited for: 3 -> 0; matrix products, arithmetic and copies ran while one was open for 0% -> 0% of each run, Pallas kernels for 0% -> 0%
where the time goes in v1:
time: 122 us; the launch traced here: 121 us
  Pallas kernels  119 us (98%)
  other arithmetic  1.36 us (1%)
    pallas_call x1, Pallas kernels, local(): pl.pallas_call(mlp_and_sae, out_shape=full + full + [shape((512, 512), BF...  105 us
    pallas_call x1, Pallas kernels, local(): pl.pallas_call(gradients, out_shape=[shape((D, 512), BF16), shape((512, D...  14.5 us

profile of v1, /device:TPU:1, one launch (start us, length us, event | category | flops | bytes accessed | tf_op | source)
XLA Modules:
  0.0 121.3 jit_solution(10943591675111023568)
XLA Ops:
  0.6 104.7 %forward.1 = (bf16[2,4,4,4,16,256]{5,4,3,2,1,0:T(8,128)(2,1)}, bf16[2,4,4,4,16,256]{5,4,3,2,1,0:T(8,128)(2,1)}, bf16[2,4,4,4,16,384]{5,4,3,2,1,0:T(8,128)(2,1)},...) custom-call(bf16[112,128]{1,0:T(8,128)(2,1)} %bitcast.13, ...), custom_call_target="tpu_custom_call" | custom-call | tf_op jit(solution)/shard_map/forward/pallas_call | solution.py:436
  105.4 14.5 %gradients.1 = (bf16[3584,512]{1,0:T(8,128)(2,1)}, bf16[512,3584]{1,0:T(8,128)(2,1)}, f32[1,512]{1,0:T(1,128)}, f32[1,512]{1,0:T(1,128)}, f32[1,3584]{1,0:T(1,128)}, /*index=5*/f32[1,1]{1,0:T(1,128)}) custom-call(f32[1,512]{1,0:T(1,128)} %bitcast.18, f32[8,128]{1,0:T(8,128)} %get-tuple-element.21.gate_in, ...), custom_call_target="tpu_custom_call" | custom-call | tf_op jit(solution)/shard_map/gradients/pallas_call | solution.py:471
  119.9 1.4 %reduce = f32[3584]{0:T(1024)} reduce(f32[1,3584]{1,0:T(1,128)} %get-tuple-element.35, f32[]{:T(128)} %constant.1), dimensions={0}, to_apply=%get-tuple-element.35.reduce_sub_computation | reduce | bytes 28676 | tf_op jit(solution)/shard_map/gradients/pallas_call | solution.py:471

commit v2 on v1

v2 whole, which is shorter than its diff:
```python
import jax
import jax.numpy as jnp
from jax import lax
from jax.experimental import pallas as pl
from jax.experimental.pallas import tpu as pltpu
from jax.sharding import PartitionSpec as P

norm_eps = 1e-06
gate_band = 0.1
sparsity_coef = 0.05

MESH = pl.DeviceIdType.MESH
F32 = jnp.float32
BF16 = jnp.bfloat16

D = 3584
QUARTER = 896
WIDTHS = (256, 256, 384)
OFFSETS = (0, 256, 512)
ORDERS = ("xyz", "yzx", "zxy")
PIECES = (0, 1, 2)


def coordinates():
    y = lax.axis_index("dp")
    m = lax.axis_index("mp")
    return {"x": m // 8, "y": y, "z": (m // 2) % 4, "c": m % 2}


def device(at):
    return (at["y"], (at["x"] * 4 + at["z"]) * 2 + at["c"])


def moved(at, axis, steps):
    there = dict(at)
    there[axis] = (at[axis] + steps) % (2 if axis == "c" else 4)
    return there


def grid_index(at, gathered):
    return tuple(slice(None) if a in gathered else at[a] for a in "yxz")


def halves(at, order, value, half):
    there = dict(at)
    there[order[2]] = value
    first = [a for a in "yxz" if a != order[2]][0]
    return tuple(
        there[a] if a == order[2] else slice(2 * half, 2 * half + 2) if a == first else slice(None)
        for a in "yxz"
    )


def forward(
    resid, pre_gain, post_gain, b_dec, b_enc, threshold,
    wg_hbm, wu_hbm, wd_hbm, we_hbm, wdec_hbm,
    err_out, lt_out, featt_out, gpre_out, gate_out, benc_out, thresh_out,
    wg, wu, wd, we, wdec, gath, norm_t, hidden, bp, bp_in, bs, b_in, sq, sq_in,
    l0, l1, l2, feat, feat_t, pre, soft_s, slope_s, gfeat, gpre, lt,
    p0, p1, p2, pin0, pin1, pin2, s0, s1, s2,
    ra0, ra1, ra2, rl0, rl1, rl2, ro0, ro1, ro2, sa0, sa1, sa2, rb0, rb1, rb2, sb0, sb1, sb2,
    rc0, rc1, rc2, e0, e1, e2, gsum, gin,
    wsem, asend, arecv, bcsend, bcrecv, bsend, brecv, sqsend, sqrecv,
    dsend, drecv, dlsend, dlrecv, dcsend, dcrecv, pcsend, pcrecv, fsend, frecv, rsend, rrecv,
    esend, erecv, elsend, elrecv, ecsend, ecrecv, gsend, grecv, osem,
):
    at = coordinates()
    x, y, z, c = at["x"], at["y"], at["z"], at["c"]
    sibling = device(moved(at, "c", 1))
    layer = (l0, l1, l2)
    part = (p0, p1, p2)
    part_in = (pin0, pin1, pin2)
    total = (s0, s1, s2)
    in_a, relay_in, relay_out, sum_a = (ra0, ra1, ra2), (rl0, rl1, rl2), (ro0, ro1, ro2), (sa0, sa1, sa2)
    in_b, sum_b = (rb0, rb1, rb2), (sb0, sb1, sb2)
    in_c = (rc0, rc1, rc2)
    err = (e0, e1, e2)

    loads = [
        pltpu.make_async_copy(src, dst, wsem.at[i])
        for i, (src, dst) in enumerate(
            ((wg_hbm, wg), (wu_hbm, wu), (wd_hbm, wd), (we_hbm, we), (wdec_hbm, wdec))
        )
    ]

    plane = [(i, j) for i in range(4) for j in range(4) if i or j]
    barrier = pltpu.get_barrier_semaphore()
    greeted = [moved(moved(at, "x", i), "z", j) for i, j in plane]
    greeted += [moved(at, "y", k) for k in (1, 2, 3)] + [moved(at, "c", 1)]
    for there in greeted:
        pl.semaphore_signal(barrier, inc=1, device_id=device(there), device_id_type=MESH)
    pl.semaphore_wait(barrier, len(greeted))

    unsent = []

    def remote(src, dst, send, recv, there):
        copy = pltpu.make_async_remote_copy(
            src_ref=src, dst_ref=dst, send_sem=send, recv_sem=recv,
            device_id=there, device_id_type=MESH,
        )
        copy.start()
        unsent.append(copy)
        return copy

    copies = []
    for n, (i, j) in enumerate(plane):
        there = moved(moved(at, "x", i), "z", j)
        copies.append(remote(resid, gath.at[x, z, c], asend.at[n], arecv.at[n], device(there)))
    loads[0].start()
    loads[1].start()
    gath[x, z, c] = resid[...]
    for copy in copies:
        copy.wait_recv()
    copy = remote(gath.at[:, :, c], gath.at[:, :, c], asend.at[15], arecv.at[15], sibling)
    loads[2].start()
    copy.wait_recv()

    squares = jnp.zeros((1, 128), F32)
    for i in range(4):
        for j in range(4):
            rows = gath[i, j].astype(F32).reshape(224, 128)
            squares = squares + jnp.sum(rows * rows, axis=0, keepdims=True)
    scale = lax.rsqrt(squares / D + norm_eps)
    gains = jnp.concatenate([pre_gain[...], jnp.zeros((100, 128), F32)], axis=0).T
    everything = gath[...].reshape(D, 128)
    for k in range(28):
        rows = everything[k * 128:(k + 1) * 128].astype(F32)
        norm_t[k * 128:(k + 1) * 128, :] = (rows * scale * gains[:, k:k + 1]).astype(BF16)

    loads[0].wait()
    loads[1].wait()
    gate = jnp.dot(wg[...], norm_t[...], preferred_element_type=F32)
    up = jnp.dot(wu[...], norm_t[...], preferred_element_type=F32)
    hidden[...] = (jax.nn.gelu(gate, approximate=True) * up).T.astype(BF16)

    loads[2].wait()
    copies = []
    for q in range(4):
        own = jnp.dot(hidden[...], wd[:, q * QUARTER:(q + 1) * QUARTER], preferred_element_type=F32)
        bp[:, :, q] = own.reshape(2, 4, 16, QUARTER)
        copies.append(remote(bp.at[1 - c, :, q], bp_in.at[:, q], bcsend.at[q], bcrecv.at[q], sibling))
    for q, copy in enumerate(copies):
        copy.wait_recv()
        bs[:, q] = (bp[c, :, q] + bp_in[:, q]).astype(BF16)
    copies = []
    for n, (i, j) in enumerate(plane):
        there = moved(moved(at, "x", i), "z", j)
        copies.append(
            remote(bs.at[there["x"], there["z"]], b_in.at[n], bsend.at[n], brecv.at[n], device(there))
        )
    loads[3].start()
    pick = lax.broadcasted_iota(jnp.int32, (16, 128), 0) + (c * 64 + x * 16)
    pick = (lax.broadcasted_iota(jnp.int32, (16, 128), 1) == pick).astype(BF16)
    mine = lax.dot_general(
        pick, own_rows(gath, z), (((1,), (1,)), ((), ())), preferred_element_type=F32
    )
    block = bp[c, x, z] + bp_in[x, z]
    for n, copy in enumerate(copies):
        copy.wait_recv()
        block = block + b_in[n].astype(F32)
    sums = jnp.broadcast_to(jnp.sum(block * block, axis=1, keepdims=True), (16, 128))
    sq[...] = sums
    copies = [
        remote(sq, sq_in.at[k - 1], sqsend.at[k - 1], sqrecv.at[k - 1], device(moved(at, "z", k)))
        for k in (1, 2, 3)
    ]
    for k, copy in enumerate(copies):
        copy.wait_recv()
        sums = sums + sq_in[k]
    row_scale = lax.rsqrt(sums[:, :1] / D + norm_eps)
    gain = lane_row(post_gain, z)
    block = mine + block * row_scale * gain
    for p in PIECES:
        layer[p][c, y, x, z] = block[:, OFFSETS[p]:OFFSETS[p] + WIDTHS[p]].astype(BF16)

    def gather(arrays, send, recv, lsend, lrecv, csend, crecv, use):
        stage, last, across = {}, {}, {}
        for step in range(2):
            for p in PIECES:
                order = ORDERS[p]
                if step:
                    for copy in stage[p]:
                        copy.wait_recv()
                here = arrays[p].at[(c,) + grid_index(at, order[:step])]
                stage[p] = [
                    remote(here, here, send.at[step, p, k - 1], recv.at[step, p, k - 1],
                           device(moved(at, order[step], k)))
                    for k in (1, 2, 3)
                ]

        def pass_on(p, owner, half, steps, n):
            order = ORDERS[p]
            value = moved(at, order[2], owner)[order[2]]
            ref = arrays[p].at[(c,) + halves(at, order, value, half)]
            return remote(ref, ref, lsend.at[p, n], lrecv.at[p, n], device(moved(at, order[2], steps)))

        def cross(p, owner):
            ref = arrays[p].at[(c,) + grid_index(moved(at, ORDERS[p][2], owner), ORDERS[p][:2])]
            across[p].append(remote(ref, ref, csend.at[p, owner], crecv.at[p, owner], sibling))

        for p in PIECES:
            for copy in stage[p]:
                copy.wait_recv()
            last[p] = [
                pass_on(p, 0, 0, 1, 0), pass_on(p, 0, 1, 3, 1),
                pass_on(p, 0, 1, 1, 2), pass_on(p, 0, 0, 3, 3),
            ]
            across[p] = []
            cross(p, 0)
        for p in PIECES:
            last[p][0].wait_recv()
            last[p].append(pass_on(p, 3, 0, 1, 4))
            last[p][1].wait_recv()
            last[p].append(pass_on(p, 1, 1, 3, 5))
        for p in PIECES:
            last[p][2].wait_recv()
            cross(p, 3)
            last[p][3].wait_recv()
            cross(p, 1)

        def finish(p):
            last[p][4].wait_recv()
            last[p][5].wait_recv()
            cross(p, 2)

        def use_all(p):
            for copy in across[p]:
                copy.wait_recv()
            use(p)

        finish(0)
        finish(1)
        use_all(0)
        finish(2)
        use_all(1)
        use_all(2)

    def encode(p):
        for q in range(4):
            low = q * QUARTER + OFFSETS[p]
            rows = layer[p][:, :, :, q].reshape(512, WIDTHS[p])
            more = jnp.dot(rows, we[low:low + WIDTHS[p], :], preferred_element_type=F32)
            if p == 0 and q == 0:
                pre[...] = b_enc[...] + more
            else:
                pre[...] += more

    loads[3].wait()
    loads[4].start()
    gather(layer, dsend, drecv, dlsend, dlrecv, dcsend, dcrecv, encode)

    pre_act = pre[...]
    soft = jax.nn.sigmoid((pre_act - threshold[...]) / gate_band)
    soft_s[...] = soft
    feat[...] = (pre_act * soft).astype(BF16)

    loads[4].wait()

    def partial(p, half):
        rows = feat[pl.ds(pl.multiple_of(half * 256, 256), 256), :]
        for q in range(4):
            low = q * QUARTER + OFFSETS[p]
            value = jnp.dot(rows, wdec[:, low:low + WIDTHS[p]], preferred_element_type=F32)
            part[p][half, :, :, q] = value.astype(BF16).reshape(4, 4, 16, WIDTHS[p])

    copies = []
    for p in PIECES:
        partial(p, 1 - c)
        copies.append(remote(part[p].at[1 - c], part_in[p], pcsend.at[p], pcrecv.at[p], sibling))
    stage = {}
    for p in PIECES:
        partial(p, c)
        copies[p].wait_recv()
        for i in range(4):
            total[p][i] = (part[p][c, i].astype(F32) + part_in[p][i].astype(F32)).astype(BF16)
        order = ORDERS[p]
        up, down = device(moved(at, order[2], 1)), device(moved(at, order[2], 3))
        value = {k: moved(at, order[2], k)[order[2]] for k in range(4)}

        def piece(k, half):
            return total[p].at[halves(at, order, value[k], half)]

        def first(src, dst, n, there):
            return remote(src, dst, fsend.at[p, n], frecv.at[p, n], there)

        stage[p] = [
            first(piece(2, 0), relay_in[p].at[0], 0, up),
            first(piece(2, 1), relay_in[p].at[1], 1, down),
            first(piece(1, 1), in_a[p].at[0, 2:4], 2, up),
            first(piece(3, 0), in_a[p].at[1, 0:2], 3, down),
        ]
    soft = soft_s[...]
    gate_sum = jnp.broadcast_to(jnp.sum(soft).reshape(1, 1), (8, 128))
    gsum[0] = gate_sum
    gate_copies = [remote(gsum.at[0], gin.at[9], gsend.at[9], grecv.at[9], sibling)]
    for p in PIECES:
        order = ORDERS[p]
        up, down = moved(at, order[2], 1), moved(at, order[2], 3)
        for n, (there, half) in enumerate(((up, 0), (down, 1))):
            stage[p][n].wait_recv()
            own = total[p][halves(at, order, there[order[2]], half)].astype(F32)
            relay_out[p][n] = (own + relay_in[p][n].astype(F32)).astype(BF16)
            stage[p].append(
                remote(relay_out[p].at[n], in_a[p].at[n, 2 * half:2 * half + 2],
                       fsend.at[p, 4 + n], frecv.at[p, 4 + n], device(there))
            )

    gate_copies[0].wait_recv()
    gate_sum = gate_sum + gin[9]

    def gate_step(s, axis, value):
        gsum[1 + s] = value
        return [
            remote(gsum.at[1 + s], gin.at[3 * s + k - 1], gsend.at[3 * s + k - 1],
                   grecv.at[3 * s + k - 1], device(moved(at, axis, k)))
            for k in (1, 2, 3)
        ]

    def gate_finish(s, made, value):
        for k, copy in enumerate(made):
            copy.wait_recv()
            value = value + gin[3 * s + k]
        return value

    gate_copies = gate_step(0, "x", gate_sum)
    slope_s[...] = soft * (1.0 - soft) / gate_band
    feat_t[...] = feat[...].T
    outs = [pltpu.make_async_copy(feat_t, featt_out, osem.at[0])]
    outs[0].start()
    for p in PIECES:
        for q in range(4):
            low = q * QUARTER + OFFSETS[p]
            lt[low:low + WIDTHS[p], :] = layer[p][:, :, :, q].reshape(512, WIDTHS[p]).T
    outs.append(pltpu.make_async_copy(lt, lt_out, osem.at[14]))
    outs[1].start()
    for p in PIECES:
        last, second = ORDERS[p][2], ORDERS[p][1]
        for copy in stage[p][2:]:
            copy.wait_recv()
        value = total[p][grid_index(at, [a for a in "xyz" if a != last])].astype(F32)
        for k in range(2):
            value = value + in_a[p][k].astype(F32)
        sum_a[p][...] = value.astype(BF16)
        stage[p] = []
        left = [a for a in "yxz" if a != last]
        for k in (1, 2, 3):
            there = moved(at, second, k)
            src = sum_a[p].at[tuple(there[a] if a == second else slice(None) for a in left)]
            stage[p].append(
                remote(src, in_b[p].at[k - 1], rsend.at[0, p, k - 1], rrecv.at[0, p, k - 1], device(there))
            )
    gate_sum = gate_finish(0, gate_copies, gate_sum)
    gate_copies = gate_step(1, "y", gate_sum)
    for p in PIECES:
        last, second, first = ORDERS[p][2], ORDERS[p][1], ORDERS[p][0]
        for copy in stage[p]:
            copy.wait_recv()
        left = [a for a in "yxz" if a != last]
        value = sum_a[p][tuple(at[a] if a == second else slice(None) for a in left)].astype(F32)
        for k in range(3):
            value = value + in_b[p][k].astype(F32)
        sum_b[p][...] = value.astype(BF16)
        stage[p] = []
        for k in (1, 2, 3):
            there = moved(at, first, k)
            stage[p].append(
                remote(sum_b[p].at[there[first]], in_c[p].at[k - 1], rsend.at[1, p, k - 1],
                       rrecv.at[1, p, k - 1], device(there))
            )
    gate_sum = gate_finish(1, gate_copies, gate_sum)
    gate_copies = gate_step(2, "z", gate_sum)
    bias = lane_row(b_dec, z)
    for p in PIECES:
        for copy in stage[p]:
            copy.wait_recv()
        value = sum_b[p][at[ORDERS[p][0]]].astype(F32)
        for k in range(3):
            value = value + in_c[p][k].astype(F32)
        value = value + bias[:, OFFSETS[p]:OFFSETS[p] + WIDTHS[p]]
        value = value - layer[p][c, y, x, z].astype(F32)
        err[p][c, y, x, z] = value.astype(BF16)

    def back(p):
        for q in range(4):
            low = q * QUARTER + OFFSETS[p]
            out = pltpu.make_async_copy(
                err[p].at[:, :, :, q], err_out.at[:, :, :, :, low:low + WIDTHS[p]],
                osem.at[1 + 4 * p + q],
            )
            out.start()
            outs.append(out)
        for q in range(4):
            low = q * QUARTER + OFFSETS[p]
            more = lax.dot_general(
                err[p][:, :, :, q].reshape(512, WIDTHS[p]), wdec[:, low:low + WIDTHS[p]],
                (((1,), (1,)), ((), ())), preferred_element_type=F32,
            )
            if p == 0 and q == 0:
                gfeat[...] = more
            else:
                gfeat[...] += more

    gather(err, esend, erecv, elsend, elrecv, ecsend, ecrecv, back)
    gate_out[...] = gate_finish(2, gate_copies, gate_sum)
    grad_feat = gfeat[...]
    side = (grad_feat * pre[...] + sparsity_coef) * slope_s[...]
    grad_pre = grad_feat * soft_s[...] + side
    thresh_out[...] = -jnp.sum(side, axis=0, keepdims=True)
    benc_out[...] = jnp.sum(grad_pre, axis=0, keepdims=True)
    gpre[...] = grad_pre.astype(BF16)
    outs.append(pltpu.make_async_copy(gpre, gpre_out, osem.at[13]))
    outs[-1].start()
    for copy in unsent:
        copy.wait_send()
    for out in outs:
        out.wait()


def own_rows(gath, z):
    return gath[pl.ds(z, 1)].reshape(QUARTER, 128)


def lane_row(ref, z):
    rows = [ref[pl.ds(z * 7 + i, 1), :] for i in range(7)]
    return jnp.concatenate(rows, axis=1)


def gradients(featt, gpre, gate_in, benc, thresh, err, lt, wdec_grad, wenc_grad, bdec_grad, loss,
              benc_grad, thresh_grad, square):
    step = pl.program_id(0)
    rows = err[...]
    wdec_grad[...] = jnp.dot(featt[...], rows, preferred_element_type=F32).astype(BF16)
    wenc_grad[...] = jnp.dot(lt[...], gpre[...], preferred_element_type=F32).astype(BF16)
    wide = rows.astype(F32)
    bdec_grad[...] = jnp.sum(wide, axis=0, keepdims=True)
    more = jnp.sum(wide * wide, axis=0, keepdims=True)

    @pl.when(step == 0)
    def _():
        square[...] = more
        benc_grad[...] = benc[...]
        thresh_grad[...] = thresh[...]

    @pl.when(step > 0)
    def _():
        square[...] += more

    @pl.when(step == pl.num_programs(0) - 1)
    def _():
        loss[0] = (0.5 * jnp.sum(square[...]) + sparsity_coef * gate_in[0, 0]) / (512 * D)


def blocks(dtype=BF16, lead=(2, 4, 4, 4)):
    return [pltpu.VMEM(lead + (16, w), dtype) for w in WIDTHS]


STEP = 512


def local(
    residual_in, pre_gain, post_gain, w_gate, w_up, w_down, w_enc, b_enc, threshold, w_dec, b_dec
):
    vmem = pl.BlockSpec(memory_space=pltpu.VMEM)
    hbm = pl.BlockSpec(memory_space=pl.ANY)
    dma = pltpu.SemaphoreType.DMA
    shape = jax.ShapeDtypeStruct
    square = lambda dtype: pltpu.VMEM((512, 512), dtype)
    err, lt, featt, gpre, gate_total, benc, thresh = pl.pallas_call(
        forward,
        out_shape=[
            shape((2, 4, 4, 16, D), BF16), shape((D, 512), BF16), shape((512, 512), BF16),
            shape((512, 512), BF16), shape((8, 128), F32), shape((1, 512), F32), shape((1, 512), F32),
        ],
        in_specs=[vmem] * 6 + [hbm] * 5,
        out_specs=[hbm] * 4 + [vmem] * 3,
        scratch_shapes=[
            pltpu.VMEM((448, D), BF16), pltpu.VMEM((448, D), BF16), pltpu.VMEM((448, D), BF16),
            pltpu.VMEM((D, 512), BF16), pltpu.VMEM((512, D), BF16),
            pltpu.VMEM((4, 4, 2, 112, 128), BF16), pltpu.VMEM((D, 128), BF16),
            pltpu.VMEM((128, 448), BF16),
            pltpu.VMEM((2, 4, 4, 16, QUARTER), F32), pltpu.VMEM((4, 4, 16, QUARTER), F32),
            pltpu.VMEM((4, 4, 16, QUARTER), BF16), pltpu.VMEM((15, 16, QUARTER), BF16),
            pltpu.VMEM((16, 128), F32), pltpu.VMEM((3, 16, 128), F32),
            *blocks(), square(BF16), square(BF16), square(F32), square(F32), square(F32), square(F32),
            square(BF16), pltpu.VMEM((D, 512), BF16),
            *blocks(), *blocks(lead=(4, 4, 4)), *blocks(lead=(4, 4, 4)),
            *blocks(lead=(2, 4, 4)), *blocks(lead=(2, 2, 4)), *blocks(lead=(2, 2, 4)),
            *blocks(lead=(4, 4)), *blocks(lead=(3, 4)), *blocks(lead=(4,)), *blocks(lead=(3,)),
            *blocks(), pltpu.VMEM((4, 8, 128), F32), pltpu.VMEM((10, 8, 128), F32),
            dma((5,)), dma((16,)), dma((16,)), dma((4,)), dma((4,)), dma((15,)), dma((15,)),
            dma((3,)), dma((3,)),
            dma((2, 3, 3)), dma((2, 3, 3)), dma((3, 6)), dma((3, 6)), dma((3, 4)), dma((3, 4)),
            dma((3,)), dma((3,)), dma((3, 6)), dma((3, 6)), dma((2, 3, 3)), dma((2, 3, 3)),
            dma((2, 3, 3)), dma((2, 3, 3)), dma((3, 6)), dma((3, 6)), dma((3, 4)), dma((3, 4)),
            dma((10,)), dma((10,)), dma((15,)),
        ],
        compiler_params=pltpu.CompilerParams(
            collective_id=0, has_side_effects=True, vmem_limit_bytes=58 * 1024 * 1024
        ),
        name="forward",
    )(
        residual_in.T, pre_gain.reshape(28, 128), post_gain.reshape(28, 128), b_dec.reshape(28, 128),
        b_enc.reshape(1, 512), threshold.reshape(1, 512), w_gate.T, w_up.T, w_down, w_enc, w_dec,
    )
    fixed = lambda dims: pl.BlockSpec(dims, lambda i: (0, 0))
    across = pl.BlockSpec((512, STEP), lambda i: (0, i))
    along = pl.BlockSpec((STEP, 512), lambda i: (i, 0))
    grads = pl.pallas_call(
        gradients,
        grid=(D // STEP,),
        out_shape=[
            shape((512, D), BF16), shape((D, 512), BF16), shape((1, D), F32), shape((1,), F32),
            shape((1, 512), F32), shape((1, 512), F32),
        ],
        in_specs=[
            fixed((512, 512)), fixed((512, 512)), fixed((8, 128)), fixed((1, 512)), fixed((1, 512)),
            across, along,
        ],
        out_specs=[
            across, along, pl.BlockSpec((1, STEP), lambda i: (0, i)),
            pl.BlockSpec(memory_space=pltpu.SMEM), fixed((1, 512)), fixed((1, 512)),
        ],
        scratch_shapes=[pltpu.VMEM((1, STEP), F32)],
        compiler_params=pltpu.CompilerParams(vmem_limit_bytes=60 * 1024 * 1024),
        name="gradients",
    )(featt, gpre, gate_total, benc, thresh, err.reshape(512, D), lt)
    return (
        grads[3].reshape(()), grads[1], grads[0], grads[4].reshape(512), grads[5].reshape(512),
        grads[2].reshape(D),
    )


def solution(mesh):
    placed = (
        P("dp", "mp"),
        P(),
        P(),
        P(None, "mp"),
        P(None, "mp"),
        P("mp", None),
        P(None, ("dp", "mp")),
        P(("dp", "mp")),
        P(("dp", "mp")),
        P(("dp", "mp"), None),
        P(),
    )
    return jax.shard_map(
        local,
        mesh=mesh,
        in_specs=placed,
        out_specs=(
            P(),
            P(None, ("dp", "mp")),
            P(("dp", "mp"), None),
            P(("dp", "mp")),
            P(("dp", "mp")),
            P(),
        ),
        check_vma=False,
    )
```

time: 122 us -> 116 us (0.951)
  Pallas kernels: 119 us -> 114 us
    pallas_call x2, Pallas kernels: 119 us -> 114 us  [the longest x1 103 us: local(): pl.pallas_call(forward, out_shape=[shape((2, 4, 4, 16, D), BF16), shape((...]
where the time goes in v2:
time: 116 us
  Pallas kernels  114 us (98%)
  other arithmetic  1.36 us (1%)
    pallas_call x1, Pallas kernels, local(): pl.pallas_call(forward, out_shape=[shape((2, 4, 4, 16, D), BF16), shape((...  103 us
    pallas_call x1, Pallas kernels, local(): pl.pallas_call(gradients, grid=(D // STEP,), out_shape=[shape((512, D), B...  10.5 us

profile of v2, /device:TPU:1, one launch (start us, length us, event | category | flops | bytes accessed | tf_op | source)
XLA Modules:
  0.0 115.5 jit_solution(17294977924831459746)
XLA Ops:
  0.6 103.0 %forward.1 = (bf16[2,4,4,16,3584]{4,3,2,1,0:T(8,128)(2,1)}, bf16[3584,512]{1,0:T(8,128)(2,1)}, bf16[512,512]{1,0:T(8,128)(2,1)}, bf16[512,512]{1,0:T(8,128)(2,1)...) custom-call(bf16[112,128]{1,0:T(8,128)(2,1)} %bitcast.15, f32[28,128]{1,0:T(8,128)} %bitcast.16, ...), custom_call_target="tpu_custom_call" | custom-call | tf_op jit(solution)/shard_map/forward/pallas_call | solution.py:468
  103.7 10.5 %gradients.1 = (bf16[512,3584]{1,0:T(8,128)(2,1)}, bf16[3584,512]{1,0:T(8,128)(2,1)}, f32[1,3584]{1,0:T(1,128)}, f32[1]{0:T(128)}, f32[1,512]{1,0:T(1,128)}, /*index=5*/f32[1,512]{1,0:T(1,128)}) custom-call(bf16[512,512]{1,0:T(8,128)(2,1)} %get-tuple-element.19.featt, bf16[512,512]{1,0:T(8,128)(2,1)} %get-tuple-element.20.gpre, ...), custom_call_target="tpu_custom_call" | custom-call | tf_op jit(solution)/shard_map/gradients/pallas_call | solution.py:508
  114.2 1.4 %reduce = f32[3584]{0:T(1024)} reduce(f32[1,3584]{1,0:T(1,128)} %get-tuple-element.31, f32[]{:T(128)} %constant.1), dimensions={0}, to_apply=%get-tuple-element.31.reduce_sub_computation | reduce | bytes 28676 | tf_op jit(solution)/shard_map/gradients/pallas_call | solution.py:508

commit v3 on v2

--- a/solution.py
+++ b/solution.py
@@ -52,10 +52,10 @@
 
 
 def forward(
-    resid, pre_gain, post_gain, b_dec, b_enc, threshold,
+    resid, pre_gain_hbm, post_gain_hbm, b_dec_hbm, b_enc_hbm, threshold_hbm,
     wg_hbm, wu_hbm, wd_hbm, we_hbm, wdec_hbm,
     err_out, lt_out, featt_out, gpre_out, gate_out, benc_out, thresh_out,
-    wg, wu, wd, we, wdec, gath, norm_t, hidden, bp, bp_in, bs, b_in, sq, sq_in,
+    pre_gain, post_gain, b_dec, b_enc, threshold, wg, wu, wd, we, wdec, gath, norm_t, hidden, bp, bp_in, bs, b_in, sq, sq_in,
     l0, l1, l2, feat, feat_t, pre, soft_s, slope_s, gfeat, gpre, lt,
     p0, p1, p2, pin0, pin1, pin2, s0, s1, s2,
     ra0, ra1, ra2, rl0, rl1, rl2, ro0, ro1, ro2, sa0, sa1, sa2, rb0, rb1, rb2, sb0, sb1, sb2,
@@ -79,9 +79,14 @@
     loads = [
         pltpu.make_async_copy(src, dst, wsem.at[i])
         for i, (src, dst) in enumerate(
-            ((wg_hbm, wg), (wu_hbm, wu), (wd_hbm, wd), (we_hbm, we), (wdec_hbm, wdec))
+            ((wg_hbm, wg), (wu_hbm, wu), (wd_hbm, wd), (we_hbm, we), (wdec_hbm, wdec),
+             (pre_gain_hbm, pre_gain), (post_gain_hbm, post_gain), (b_dec_hbm, b_dec),
+             (b_enc_hbm, b_enc), (threshold_hbm, threshold),
+             (resid, gath.at[at["x"], at["z"], at["c"]]))
         )
     ]
+    for load in loads[5:]:
+        load.start()
 
     plane = [(i, j) for i in range(4) for j in range(4) if i or j]
     barrier = pltpu.get_barrier_semaphore()
@@ -108,7 +113,8 @@
         copies.append(remote(resid, gath.at[x, z, c], asend.at[n], arecv.at[n], device(there)))
     loads[0].start()
     loads[1].start()
-    gath[x, z, c] = resid[...]
+    for load in loads[5:]:
+        load.wait()
     for copy in copies:
         copy.wait_recv()
     copy = remote(gath.at[:, :, c], gath.at[:, :, c], asend.at[15], arecv.at[15], sibling)
@@ -173,12 +179,12 @@
     for p in PIECES:
         layer[p][c, y, x, z] = block[:, OFFSETS[p]:OFFSETS[p] + WIDTHS[p]].astype(BF16)
 
-    def gather(arrays, send, recv, lsend, lrecv, csend, crecv, use):
+    def gather(arrays, send, recv, lsend, lrecv, csend, crecv, use, known=0):
         stage, last, across = {}, {}, {}
-        for step in range(2):
+        for step in range(known, 2):
             for p in PIECES:
                 order = ORDERS[p]
-                if step:
+                if step > known:
                     for copy in stage[p]:
                         copy.wait_recv()
                 here = arrays[p].at[(c,) + grid_index(at, order[:step])]
@@ -223,27 +229,27 @@
             last[p][5].wait_recv()
             cross(p, 2)
 
-        def use_all(p):
+        finish(0)
+        finish(1)
+        use(0, c)
+        finish(2)
+        use(1, c)
+        use(2, c)
+        for p in PIECES:
             for copy in across[p]:
                 copy.wait_recv()
-            use(p)
-
-        finish(0)
-        finish(1)
-        use_all(0)
-        finish(2)
-        use_all(1)
-        use_all(2)
-
-    def encode(p):
+            use(p, 1 - c)
+
+    def encode(p, half):
+        tokens = pl.ds(pl.multiple_of(half * 256, 256), 256)
         for q in range(4):
             low = q * QUARTER + OFFSETS[p]
-            rows = layer[p][:, :, :, q].reshape(512, WIDTHS[p])
+            rows = layer[p][half, :, :, q].reshape(256, WIDTHS[p])
             more = jnp.dot(rows, we[low:low + WIDTHS[p], :], preferred_element_type=F32)
             if p == 0 and q == 0:
-                pre[...] = b_enc[...] + more
+                pre[tokens, :] = b_enc[...] + more
             else:
-                pre[...] += more
+                pre[tokens, :] += more
 
     loads[3].wait()
     loads[4].start()
@@ -331,7 +337,7 @@
         for q in range(4):
             low = q * QUARTER + OFFSETS[p]
             lt[low:low + WIDTHS[p], :] = layer[p][:, :, :, q].reshape(512, WIDTHS[p]).T
-    outs.append(pltpu.make_async_copy(lt, lt_out, osem.at[14]))
+    outs.append(pltpu.make_async_copy(lt, lt_out, osem.at[1]))
     outs[1].start()
     for p in PIECES:
         last, second = ORDERS[p][2], ORDERS[p][1]
@@ -359,48 +365,54 @@
         value = sum_a[p][tuple(at[a] if a == second else slice(None) for a in left)].astype(F32)
         for k in range(3):
             value = value + in_b[p][k].astype(F32)
-        sum_b[p][...] = value.astype(BF16)
+        value = value.astype(BF16)
+        sum_b[p][...] = value
+        in_c[p][at[first]] = value
         stage[p] = []
         for k in (1, 2, 3):
-            there = moved(at, first, k)
             stage[p].append(
-                remote(sum_b[p].at[there[first]], in_c[p].at[k - 1], rsend.at[1, p, k - 1],
-                       rrecv.at[1, p, k - 1], device(there))
+                remote(sum_b[p], in_c[p].at[at[first]], rsend.at[1, p, k - 1],
+                       rrecv.at[1, p, k - 1], device(moved(at, first, k)))
             )
     gate_sum = gate_finish(1, gate_copies, gate_sum)
     gate_copies = gate_step(2, "z", gate_sum)
-    bias = lane_row(b_dec, z)
-    for p in PIECES:
+    for p in PIECES:
+        first = ORDERS[p][0]
         for copy in stage[p]:
             copy.wait_recv()
-        value = sum_b[p][at[ORDERS[p][0]]].astype(F32)
-        for k in range(3):
-            value = value + in_c[p][k].astype(F32)
-        value = value + bias[:, OFFSETS[p]:OFFSETS[p] + WIDTHS[p]]
-        value = value - layer[p][c, y, x, z].astype(F32)
-        err[p][c, y, x, z] = value.astype(BF16)
-
-    def back(p):
+        for i in range(4):
+            value = in_c[p][0, i].astype(F32)
+            for k in (1, 2, 3):
+                value = value + in_c[p][k, i].astype(F32)
+            there = dict(at)
+            there[first] = i
+            bias = lane_row(b_dec, there["z"])
+            value = value + bias[:, OFFSETS[p]:OFFSETS[p] + WIDTHS[p]]
+            value = value - layer[p][c, there["y"], there["x"], there["z"]].astype(F32)
+            err[p][c, there["y"], there["x"], there["z"]] = value.astype(BF16)
+
+    def back(p, half):
+        tokens = pl.ds(pl.multiple_of(half * 256, 256), 256)
         for q in range(4):
             low = q * QUARTER + OFFSETS[p]
             out = pltpu.make_async_copy(
-                err[p].at[:, :, :, q], err_out.at[:, :, :, :, low:low + WIDTHS[p]],
-                osem.at[1 + 4 * p + q],
+                err[p].at[half, :, :, q], err_out.at[half, :, :, :, low:low + WIDTHS[p]],
+                osem.at[len(outs)],
             )
             out.start()
             outs.append(out)
         for q in range(4):
             low = q * QUARTER + OFFSETS[p]
             more = lax.dot_general(
-                err[p][:, :, :, q].reshape(512, WIDTHS[p]), wdec[:, low:low + WIDTHS[p]],
+                err[p][half, :, :, q].reshape(256, WIDTHS[p]), wdec[:, low:low + WIDTHS[p]],
                 (((1,), (1,)), ((), ())), preferred_element_type=F32,
             )
             if p == 0 and q == 0:
-                gfeat[...] = more
+                gfeat[tokens, :] = more
             else:
-                gfeat[...] += more
-
-    gather(err, esend, erecv, elsend, elrecv, ecsend, ecrecv, back)
+                gfeat[tokens, :] += more
+
+    gather(err, esend, erecv, elsend, elrecv, ecsend, ecrecv, back, 1)
     gate_out[...] = gate_finish(2, gate_copies, gate_sum)
     grad_feat = gfeat[...]
     side = (grad_feat * pre[...] + sparsity_coef) * slope_s[...]
@@ -408,7 +420,7 @@
     thresh_out[...] = -jnp.sum(side, axis=0, keepdims=True)
     benc_out[...] = jnp.sum(grad_pre, axis=0, keepdims=True)
     gpre[...] = grad_pre.astype(BF16)
-    outs.append(pltpu.make_async_copy(gpre, gpre_out, osem.at[13]))
+    outs.append(pltpu.make_async_copy(gpre, gpre_out, osem.at[26]))
     outs[-1].start()
     for copy in unsent:
         copy.wait_send()
@@ -432,7 +444,9 @@
     wdec_grad[...] = jnp.dot(featt[...], rows, preferred_element_type=F32).astype(BF16)
     wenc_grad[...] = jnp.dot(lt[...], gpre[...], preferred_element_type=F32).astype(BF16)
     wide = rows.astype(F32)
-    bdec_grad[...] = jnp.sum(wide, axis=0, keepdims=True)
+    sums = jnp.sum(wide, axis=0, keepdims=True)
+    for i in range(STEP // 128):
+        bdec_grad[pl.ds(step * (STEP // 128) + i, 1), :] = sums[:, i * 128:(i + 1) * 128]
     more = jnp.sum(wide * wide, axis=0, keepdims=True)
 
     @pl.when(step == 0)
@@ -471,9 +485,10 @@
             shape((2, 4, 4, 16, D), BF16), shape((D, 512), BF16), shape((512, 512), BF16),
             shape((512, 512), BF16), shape((8, 128), F32), shape((1, 512), F32), shape((1, 512), F32),
         ],
-        in_specs=[vmem] * 6 + [hbm] * 5,
+        in_specs=[hbm] * 11,
         out_specs=[hbm] * 4 + [vmem] * 3,
         scratch_shapes=[
+            *[pltpu.VMEM((28, 128), F32)] * 3, *[pltpu.VMEM((1, 512), F32)] * 2,
             pltpu.VMEM((448, D), BF16), pltpu.VMEM((448, D), BF16), pltpu.VMEM((448, D), BF16),
             pltpu.VMEM((D, 512), BF16), pltpu.VMEM((512, D), BF16),
             pltpu.VMEM((4, 4, 2, 112, 128), BF16), pltpu.VMEM((D, 128), BF16),
@@ -485,14 +500,14 @@
             square(BF16), pltpu.VMEM((D, 512), BF16),
             *blocks(), *blocks(lead=(4, 4, 4)), *blocks(lead=(4, 4, 4)),
             *blocks(lead=(2, 4, 4)), *blocks(lead=(2, 2, 4)), *blocks(lead=(2, 2, 4)),
-            *blocks(lead=(4, 4)), *blocks(lead=(3, 4)), *blocks(lead=(4,)), *blocks(lead=(3,)),
+            *blocks(lead=(4, 4)), *blocks(lead=(3, 4)), *blocks(lead=(4,)), *blocks(lead=(4, 4)),
             *blocks(), pltpu.VMEM((4, 8, 128), F32), pltpu.VMEM((10, 8, 128), F32),
-            dma((5,)), dma((16,)), dma((16,)), dma((4,)), dma((4,)), dma((15,)), dma((15,)),
+            dma((11,)), dma((16,)), dma((16,)), dma((4,)), dma((4,)), dma((15,)), dma((15,)),
             dma((3,)), dma((3,)),
             dma((2, 3, 3)), dma((2, 3, 3)), dma((3, 6)), dma((3, 6)), dma((3, 4)), dma((3, 4)),
             dma((3,)), dma((3,)), dma((3, 6)), dma((3, 6)), dma((2, 3, 3)), dma((2, 3, 3)),
             dma((2, 3, 3)), dma((2, 3, 3)), dma((3, 6)), dma((3, 6)), dma((3, 4)), dma((3, 4)),
-            dma((10,)), dma((10,)), dma((15,)),
+            dma((10,)), dma((10,)), dma((27,)),
         ],
         compiler_params=pltpu.CompilerParams(
             collective_id=0, has_side_effects=True, vmem_limit_bytes=58 * 1024 * 1024
@@ -509,7 +524,7 @@
         gradients,
         grid=(D // STEP,),
         out_shape=[
-            shape((512, D), BF16), shape((D, 512), BF16), shape((1, D), F32), shape((1,), F32),
+            shape((512, D), BF16), shape((D, 512), BF16), shape((28, 128), F32), shape((1,), F32),
             shape((1, 512), F32), shape((1, 512), F32),
         ],
         in_specs=[
@@ -517,7 +532,7 @@
             across, along,
         ],
         out_specs=[
-            across, along, pl.BlockSpec((1, STEP), lambda i: (0, i)),
+            across, along, fixed((28, 128)),
             pl.BlockSpec(memory_space=pltpu.SMEM), fixed((1, 512)), fixed((1, 512)),
         ],
         scratch_shapes=[pltpu.VMEM((1, STEP), F32)],

time: 116 us -> 112 us (0.966)
  Pallas kernels: 114 us -> 111 us
  other arithmetic: 1.36 us -> 0 us
    pallas_call x1, Pallas kernels: 103 us -> 101 us  [local(): pl.pallas_call(forward, out_shape=[shape((2, 4, 4, 16, D), BF16), shape((...]
    pallas_call x1 -> x0, other arithmetic: 1.36 us -> none  [local(): pl.pallas_call(gradients, grid=(D // STEP,), out_shape=[shape((512, D), B...]
where the time goes in v3:
time: 112 us
  Pallas kernels  111 us (99%)
    pallas_call x1, Pallas kernels, local(): pl.pallas_call(forward, out_shape=[shape((2, 4, 4, 16, D), BF16), shape((...  101 us
    pallas_call x1, Pallas kernels, local(): pl.pallas_call(gradients, grid=(D // STEP,), out_shape=[shape((512, D), B...  10.5 us

profile of v3, /device:TPU:1, one launch (start us, length us, event | category | flops | bytes accessed | tf_op | source)
XLA Modules:
  0.0 112.1 jit_solution(190854585948094223)
XLA Ops:
  0.6 100.9 %forward.1 = (bf16[2,4,4,16,3584]{4,3,2,1,0:T(8,128)(2,1)}, bf16[3584,512]{1,0:T(8,128)(2,1)}, bf16[512,512]{1,0:T(8,128)(2,1)}, bf16[512,512]{1,0:T(8,128)(2,1)...) custom-call(bf16[112,128]{1,0:T(8,128)(2,1)} %bitcast.16, f32[28,128]{1,0:T(8,128)} %bitcast.17, ...), custom_call_target="tpu_custom_call" | custom-call | tf_op jit(solution)/shard_map/forward/pallas_call | solution.py:482
  101.6 10.5 %gradients.1 = (bf16[512,3584]{1,0:T(8,128)(2,1)}, bf16[3584,512]{1,0:T(8,128)(2,1)}, f32[28,128]{1,0:T(8,128)}, f32[1]{0:T(128)}, f32[1,512]{1,0:T(1,128)}, /*index=5*/f32[1,512]{1,0:T(1,128)}) custom-call(bf16[512,512]{1,0:T(8,128)(2,1)} %get-tuple-element.19.featt, bf16[512,512]{1,0:T(8,128)(2,1)} %get-tuple-element.20.gpre, ...), custom_call_target="tpu_custom_call" | custom-call | tf_op jit(solution)/shard_map/gradients/pallas_call | solution.py:523

commit v4 on v3

--- a/solution.py
+++ b/solution.py
@@ -19,6 +19,7 @@
 OFFSETS = (0, 256, 512)
 ORDERS = ("xyz", "yzx", "zxy")
 PIECES = (0, 1, 2)
+WIDEST_FIRST = (2, 0, 1)
 
 
 def coordinates():
@@ -115,11 +116,16 @@
     loads[1].start()
     for load in loads[5:]:
         load.wait()
-    for copy in copies:
+    across = []
+    for n, i in enumerate((0, 1, 3, 2)):
+        for (k, _), copy in zip(plane, copies):
+            if k == i:
+                copy.wait_recv()
+        ref = gath.at[moved(at, "x", 4 - i)["x"], :, c]
+        across.append(remote(ref, ref, asend.at[15 + n], arecv.at[15 + n], sibling))
+    loads[2].start()
+    for copy in across:
         copy.wait_recv()
-    copy = remote(gath.at[:, :, c], gath.at[:, :, c], asend.at[15], arecv.at[15], sibling)
-    loads[2].start()
-    copy.wait_recv()
 
     squares = jnp.zeros((1, 128), F32)
     for i in range(4):
@@ -182,7 +188,7 @@
     def gather(arrays, send, recv, lsend, lrecv, csend, crecv, use, known=0):
         stage, last, across = {}, {}, {}
         for step in range(known, 2):
-            for p in PIECES:
+            for p in WIDEST_FIRST:
                 order = ORDERS[p]
                 if step > known:
                     for copy in stage[p]:
@@ -204,7 +210,7 @@
             ref = arrays[p].at[(c,) + grid_index(moved(at, ORDERS[p][2], owner), ORDERS[p][:2])]
             across[p].append(remote(ref, ref, csend.at[p, owner], crecv.at[p, owner], sibling))
 
-        for p in PIECES:
+        for p in WIDEST_FIRST:
             for copy in stage[p]:
                 copy.wait_recv()
             last[p] = [
@@ -262,20 +268,17 @@
 
     loads[4].wait()
 
-    def partial(p, half):
-        rows = feat[pl.ds(pl.multiple_of(half * 256, 256), 256), :]
+    def partial(p):
         for q in range(4):
             low = q * QUARTER + OFFSETS[p]
-            value = jnp.dot(rows, wdec[:, low:low + WIDTHS[p]], preferred_element_type=F32)
-            part[p][half, :, :, q] = value.astype(BF16).reshape(4, 4, 16, WIDTHS[p])
-
-    copies = []
-    for p in PIECES:
-        partial(p, 1 - c)
-        copies.append(remote(part[p].at[1 - c], part_in[p], pcsend.at[p], pcrecv.at[p], sibling))
+            value = jnp.dot(feat[...], wdec[:, low:low + WIDTHS[p]], preferred_element_type=F32)
+            part[p][:, :, :, q] = value.astype(BF16).reshape(2, 4, 4, 16, WIDTHS[p])
+        copies[p] = remote(part[p].at[1 - c], part_in[p], pcsend.at[p], pcrecv.at[p], sibling)
+
+    copies = {}
     stage = {}
-    for p in PIECES:
-        partial(p, c)
+
+    def reduce_first(p):
         copies[p].wait_recv()
         for i in range(4):
             total[p][i] = (part[p][c, i].astype(F32) + part_in[p][i].astype(F32)).astype(BF16)
@@ -295,11 +298,17 @@
             first(piece(1, 1), in_a[p].at[0, 2:4], 2, up),
             first(piece(3, 0), in_a[p].at[1, 0:2], 3, down),
         ]
+    partial(2)
+    partial(0)
+    reduce_first(2)
+    partial(1)
+    reduce_first(0)
+    reduce_first(1)
     soft = soft_s[...]
     gate_sum = jnp.broadcast_to(jnp.sum(soft).reshape(1, 1), (8, 128))
     gsum[0] = gate_sum
     gate_copies = [remote(gsum.at[0], gin.at[9], gsend.at[9], grecv.at[9], sibling)]
-    for p in PIECES:
+    for p in WIDEST_FIRST:
         order = ORDERS[p]
         up, down = moved(at, order[2], 1), moved(at, order[2], 3)
         for n, (there, half) in enumerate(((up, 0), (down, 1))):
@@ -339,7 +348,7 @@
             lt[low:low + WIDTHS[p], :] = layer[p][:, :, :, q].reshape(512, WIDTHS[p]).T
     outs.append(pltpu.make_async_copy(lt, lt_out, osem.at[1]))
     outs[1].start()
-    for p in PIECES:
+    for p in WIDEST_FIRST:
         last, second = ORDERS[p][2], ORDERS[p][1]
         for copy in stage[p][2:]:
             copy.wait_recv()
@@ -357,7 +366,7 @@
             )
     gate_sum = gate_finish(0, gate_copies, gate_sum)
     gate_copies = gate_step(1, "y", gate_sum)
-    for p in PIECES:
+    for p in WIDEST_FIRST:
         last, second, first = ORDERS[p][2], ORDERS[p][1], ORDERS[p][0]
         for copy in stage[p]:
             copy.wait_recv()
@@ -468,7 +477,7 @@
     return [pltpu.VMEM(lead + (16, w), dtype) for w in WIDTHS]
 
 
-STEP = 512
+STEP = 1792
 
 
 def local(
@@ -502,7 +511,7 @@
             *blocks(lead=(2, 4, 4)), *blocks(lead=(2, 2, 4)), *blocks(lead=(2, 2, 4)),
             *blocks(lead=(4, 4)), *blocks(lead=(3, 4)), *blocks(lead=(4,)), *blocks(lead=(4, 4)),
             *blocks(), pltpu.VMEM((4, 8, 128), F32), pltpu.VMEM((10, 8, 128), F32),
-            dma((11,)), dma((16,)), dma((16,)), dma((4,)), dma((4,)), dma((15,)), dma((15,)),
+            dma((11,)), dma((19,)), dma((19,)), dma((4,)), dma((4,)), dma((15,)), dma((15,)),
             dma((3,)), dma((3,)),
             dma((2, 3, 3)), dma((2, 3, 3)), dma((3, 6)), dma((3, 6)), dma((3, 4)), dma((3, 4)),
             dma((3,)), dma((3,)), dma((3, 6)), dma((3, 6)), dma((2, 3, 3)), dma((2, 3, 3)),

time: 112 us -> 109 us (0.973)
  Pallas kernels: 111 us -> 108 us
    pallas_call x1, Pallas kernels: 10.5 us -> 8.62 us  [local(): pl.pallas_call(gradients, grid=(D // STEP,), out_shape=[shape((512, D), B...]
    pallas_call x1, Pallas kernels: 101 us -> 99.1 us  [local(): pl.pallas_call(forward, out_shape=[shape((2, 4, 4, 16, D), BF16), shape((...]
where the time goes in v4:
time: 109 us
  Pallas kernels  108 us (99%)
    pallas_call x1, Pallas kernels, local(): pl.pallas_call(forward, out_shape=[shape((2, 4, 4, 16, D), BF16), shape((...  99.1 us
    pallas_call x1, Pallas kernels, local(): pl.pallas_call(gradients, grid=(D // STEP,), out_shape=[shape((512, D), B...  8.62 us

profile of v4, /device:TPU:1, one launch (start us, length us, event | category | flops | bytes accessed | tf_op | source)
XLA Modules:
  0.0 108.6 jit_solution(15915259740730563149)
XLA Ops:
  0.6 99.1 %forward.1 = (bf16[2,4,4,16,3584]{4,3,2,1,0:T(8,128)(2,1)}, bf16[3584,512]{1,0:T(8,128)(2,1)}, bf16[512,512]{1,0:T(8,128)(2,1)}, bf16[512,512]{1,0:T(8,128)(2,1)...) custom-call(bf16[112,128]{1,0:T(8,128)(2,1)} %bitcast.16, f32[28,128]{1,0:T(8,128)} %bitcast.17, ...), custom_call_target="tpu_custom_call" | custom-call | tf_op jit(solution)/shard_map/forward/pallas_call | solution.py:491
  99.8 8.6 %gradients.1 = (bf16[512,3584]{1,0:T(8,128)(2,1)}, bf16[3584,512]{1,0:T(8,128)(2,1)}, f32[28,128]{1,0:T(8,128)}, f32[1]{0:T(128)}, f32[1,512]{1,0:T(1,128)}, /*index=5*/f32[1,512]{1,0:T(1,128)}) custom-call(bf16[512,512]{1,0:T(8,128)(2,1)} %get-tuple-element.19.featt, bf16[512,512]{1,0:T(8,128)(2,1)} %get-tuple-element.20.gpre, ...), custom_call_target="tpu_custom_call" | custom-call | tf_op jit(solution)/shard_map/gradients/pallas_call | solution.py:532
